TPU v7x, 256 devices: a whole 4x4x8 slice. The times are simulated.
256 devices in a mesh: branch: 2 (over core), seq: 16 (over x, z_lo), head: 8 (over y, z_hi).
Axes of the slice: x: 4, y: 4, z: 8 (z_hi: 2, z_lo: 4; z = z_hi * 4 + z_lo), core: 2. Of those that a mesh axis runs over, the one named last changes fastest.
Arguments:
- latent: float32 [8192, 3072], P(('seq', 'head')), may hold values from -8 to 8
- modulation: float32 [2, 3, 3072], P('branch'), may hold values from -1.2 to 1.2
- w_qkv: bfloat16 [3072, 24, 384], P(None, 'head'), may hold values from -5 to 5
- w_out: bfloat16 [24, 128, 3072], P('head'), may hold values from -0.5 to 0.5
- timestep: int32 [1], replicated, may hold values from 0 to 49
Outputs:
- stepped: float32 [8192, 3072], P(('seq', 'head'))
- denoised: float32 [8192, 3072], P(('seq', 'head'))
Inputs may be any that keep to these rules, and one draw needn't show every extreme that they name: `timestep`: one step index of the plan of 50 steps.
All inputs are finite; a program needn't handle non-finite values.
Results may differ from a plain program's by a relative error of at most 0.0055.
Values may be sent and summed in bfloat16 or wider, within the bound.
A program may use at most 128 MiB of HBM per device.

v0:
```python
import functools

import jax
import jax.numpy as jnp
from jax import lax
from jax.experimental import pallas as pl
from jax.experimental.pallas import tpu as pltpu
from jax.sharding import PartitionSpec as P

STEPS = 50
GUIDANCE = 6.0
SHIFT = 7.0
EPS = 1e-06
LOG2E = 1.4426950408889634
MESH = pl.DeviceIdType.MESH
F32, BF16 = jnp.float32, jnp.bfloat16

D = 3072
DH = 128
H = 3
NX, NY, NZ = 4, 4, 4
ROWS = 32
PART = ROWS // 2
CHUNK = 2 * NY * PART
WIDE = D // 2
YD = (1, 3, 2)
ZD = (2, 3, 1)


def sigma_at(step_value):
    fraction = 1.0 - step_value / STEPS
    return SHIFT * fraction / (1.0 + (SHIFT - 1.0) * fraction)


def toggled(z, k):
    if k == 1:
        return z + 1 - 2 * (z % 2)
    if k == 2:
        return z + 2 - 4 * (z // 2)
    return 3 - z


def kernel(
    lat_ref, mod_ref, wq_hbm, wo_hbm, out_ref,
    wq, wo, xh, nm, qb, kv, osend, orecv, lsend, lrecv, att, attx, gate, gatex,
    psend, precv, zsend, zrecv, fin, finx,
    w_sem, xs_sem, xr_sem, x2_sem, g_sem, qs_sem, qr_sem, q3_sem, ks_sem, kr_sem, k2_sem,
    os_sem, or_sem, ls_sem, lr_sem, as_sem, ar_sem, ps_sem, pr_sem, zs_sem, zr_sem, fs_sem, fr_sem,
):
    b, s, h = lax.axis_index("branch"), lax.axis_index("seq"), lax.axis_index("head")
    x, z, y, zh = s // NZ, s % NZ, h // 2, h % 2

    def to_y(d):
        return (b, s, ((y + d) % NY) * 2 + zh)

    def to_x(d):
        return (b, ((x + d) % NX) * NZ + z, h)

    def to_z(k):
        return (b, x * NZ + toggled(z, k), h)

    far = (b, s, h + 1 - 2 * zh)
    twin = (1 - b, s, h)
    inner = (z == 1) | (z == 2)

    def remote(src, dst, ssem, rsem, dev):
        return pltpu.make_async_remote_copy(
            src_ref=src, dst_ref=dst, send_sem=ssem, recv_sem=rsem,
            device_id=dev, device_id_type=MESH,
        )

    load_q = pltpu.make_async_copy(wq_hbm, wq, w_sem.at[0])
    load_o = pltpu.make_async_copy(wo_hbm, wo, w_sem.at[1])
    load_q.start()
    load_o.start()

    barrier = pltpu.get_barrier_semaphore()
    peers = [to_y(d) for d in YD] + [to_x(d) for d in (1, 3)] + [to_z(k) for k in ZD] + [far, twin]
    for dev in peers:
        pl.semaphore_signal(barrier, inc=1, device_id=dev, device_id_type=MESH)

    def normalise(at):
        rows = lat_ref[pl.ds(pl.multiple_of(at * ROWS, ROWS), ROWS), :]
        centred = rows - jnp.mean(rows, axis=1, keepdims=True)
        var = jnp.mean(centred * centred, axis=1, keepdims=True)
        return (centred * lax.rsqrt(var + EPS)).astype(BF16).reshape(2, PART, D)

    xh[0, :, 0, 0] = normalise(b)
    weight = jnp.where(b == 0, GUIDANCE, 1.0 - GUIDANCE).astype(F32)
    gate[...] = jnp.broadcast_to(weight * mod_ref[2], gate.shape)
    pl.semaphore_wait(barrier, len(peers))

    sends = []

    def go(copy):
        copy.start()
        sends.append(copy)
        return copy

    def x_copy(src, dst, dev):
        return go(remote(xh.at[src], xh.at[dst], xs_sem.at[dst], xr_sem.at[dst], dev))

    def modulate(dz, c, half, dy):
        rows = pl.ds(((c * 2 + half) * NY + dy) * PART, PART)

        def some(t, carry):
            cols = pl.ds(pl.multiple_of(t * tile, tile), tile)
            nm[dz, rows, cols] = (
                xh[dz, c, half, dy, :, cols].astype(F32) * (1.0 + mod_ref[1, :, cols]) + mod_ref[0, :, cols]
            ).astype(BF16)
            return carry

        lax.fori_loop(0, D // tile, some, 0)

    tile = 512
    x_in = {}

    def spread(dz, c):
        for d in (1, 3):
            x_in[dz, c, 0, d] = x_copy((dz, c, 0, 0), (dz, c, 0, d), to_y(d))

    def pass_on(dz, d, c):
        x_in[dz, c, 0, d].wait_recv()
        side = d // 2
        cols = pl.ds(side * WIDE, WIDE)
        x_in[dz, c, 0, 2, side] = go(
            remote(
                xh.at[dz, c, 0, d, :, cols],
                xh.at[dz, c, 0, 2, :, cols],
                x2_sem.at[0, dz, c, side],
                x2_sem.at[1, dz, c, side],
                to_y(d),
            )
        )
        x_in[dz, c, 1, d] = x_copy((dz, c, 0, d), (dz, c, 1, d), twin)
        modulate(dz, c, 0, d)

    def pass_last(dz, c):
        for side in range(2):
            x_in[dz, c, 0, 2, side].wait_recv()
        x_in[dz, c, 1, 2] = x_copy((dz, c, 0, 2), (dz, c, 1, 2), twin)
        modulate(dz, c, 0, 2)

    def from_far(c):
        x_in[1, c, 0, 0].wait_recv()
        spread(1, c)
        x_in[1, c, 1, 0] = x_copy((1, c, 0, 0), (1, c, 1, 0), twin)
        modulate(1, c, 0, 0)

    def from_twin(dz, c):
        for dy in (0, 1, 3, 2):
            if (dz, dy) != (0, 0):
                x_in[dz, c, 1, dy].wait_recv()
                modulate(dz, c, 1, dy)

    for c in range(2):
        x_in[1, c, 0, 0] = x_copy((0, c, 0, 0), (1, c, 0, 0), far)
        spread(0, c)
    gate_copy = go(remote(gate, gatex, g_sem.at[0], g_sem.at[1], twin))
    xh[0, :, 1, 0] = normalise(1 - b)
    for c in range(2):
        modulate(0, c, 0, 0)
        modulate(0, c, 1, 0)

    def piece(ref, m):
        return ref.at[0, m] if m < 2 else ref.at[1 if m == 2 else 0]

    def rows_of(m):
        return CHUNK if m < 2 else 2 * CHUNK

    def parts_of(m):
        return (m,) if m < 2 else (0, 1)

    q_scale = DH**-0.5 * LOG2E
    q_in, kv_in = {}, {}

    def project(m):
        dz = m // 2
        parts = (m,) if m < 2 else (0, 1)
        rows = slice(m * CHUNK, (m + 1) * CHUNK) if m < 2 else slice(0, 2 * CHUNK)

        def to_neighbours(i):
            return [
                remote(piece(kv.at[0, i], m), piece(kv.at[d, i], m), ks_sem.at[d, i, m], kr_sem.at[d, i, m], to_x(d))
                for d in (1, 3)
            ]

        def along_line(i):
            return [
                remote(piece(qb.at[0, i], m), piece(qb.at[k, i], m), qs_sem.at[k, i, m], qr_sem.at[k, i, m], to_z(k))
                for k in (2, 1, 3)
            ]

        def per_head(i, carry):
            got = jnp.dot(nm[dz, rows], wq[i, :, DH:], preferred_element_type=F32)
            for at, c in enumerate(parts):
                mine = got[at * CHUNK : (at + 1) * CHUNK]
                kv[0, i, dz, c, 0] = mine[:, :DH].T.astype(BF16)
                kv[0, i, dz, c, 1] = mine[:, DH:].astype(BF16)
            for copy in to_neighbours(i):
                copy.start()
            got = jnp.dot(nm[dz, rows], wq[i, :, :DH], preferred_element_type=F32) * q_scale
            for at, c in enumerate(parts):
                qb[0, i, dz, c] = got[at * CHUNK : (at + 1) * CHUNK].astype(BF16)
            across, near, between = along_line(i)
            across.start()
            near.start()
            pl.when(inner)(between.start)
            return carry

        lax.fori_loop(0, H, per_head, 0)
        for i in range(H):
            kv_in[1, i, m], kv_in[3, i, m] = to_neighbours(i)
            q_in[2, i, m], q_in[1, i, m], q_in[3, i, m] = along_line(i)
            sends.extend([kv_in[1, i, m], kv_in[3, i, m], q_in[2, i, m], q_in[1, i, m]])

    def relay_x(m, i):
        for d in (1, 3):
            kv_in[d, i, m].wait_recv()
            side = d // 2
            src, dst = (piece(kv.at[at, i], m).at[side] for at in (d, 2))
            kv_in[2, i, m, side] = go(
                remote(src, dst, k2_sem.at[0, i, m, side], k2_sem.at[1, i, m, side], to_x(d))
            )

    relays = []

    def relay_z(m, i):
        q_in[2, i, m].wait_recv()
        relay = remote(piece(qb.at[2, i], m), piece(qb.at[3, i], m), q3_sem.at[i, m], qr_sem.at[3, i, m], to_z(1))
        pl.when(inner)(relay.start)
        relays.append(relay)

    for c in range(2):
        pass_on(0, 1, c)
        pass_on(0, 3, c)
    from_far(0)
    pass_last(0, 0)
    from_twin(0, 0)
    load_q.wait()
    project(0)
    from_far(1)
    pass_last(0, 1)
    from_twin(0, 1)
    project(1)
    pass_on(1, 1, 0)
    pass_on(1, 3, 0)
    relay_x(0, 0)
    pass_on(1, 1, 1)
    pass_on(1, 3, 1)
    relay_x(0, 1)
    relay_x(0, 2)
    for i in range(H):
        relay_z(0, i)
    pass_last(1, 0)
    pass_last(1, 1)
    relay_x(1, 0)
    from_twin(1, 0)
    from_twin(1, 1)
    project(2)
    relay_x(1, 1)
    relay_x(1, 2)
    for i in range(H):
        relay_z(1, i)
    for i in range(H):
        relay_x(2, i)
        relay_z(2, i)

    def attend(ks, i, m):
        rows = rows_of(m)
        query = jnp.concatenate([piece(qb.at[k, i], m)[...].reshape(rows, DH) for k in ks], axis=0)
        blocks = [(d, dz) for d in range(NX) for dz in range(2)]
        scores = jnp.concatenate(
            [
                jnp.dot(
                    query,
                    jnp.concatenate([kv[d, i, dz, 0, 0], kv[d, i, dz, 1, 0]], axis=1),
                    preferred_element_type=F32,
                )
                for d, dz in blocks
            ],
            axis=1,
        )
        peak = jnp.max(scores, axis=1, keepdims=True)
        expo = jnp.exp2(scores - peak)
        total = jnp.sum(expo, axis=1, keepdims=True)
        probs = expo.astype(BF16)
        mixed = jnp.zeros((len(ks) * rows, DH), F32)
        for at, (d, dz) in enumerate(blocks):
            mixed += jnp.dot(
                probs[:, at * 2 * CHUNK : (at + 1) * 2 * CHUNK],
                jnp.concatenate([kv[d, i, dz, 0, 1], kv[d, i, dz, 1, 1]], axis=0),
                preferred_element_type=F32,
            )
        mixed = (mixed / total).astype(BF16)
        log = jnp.broadcast_to(peak + jnp.log2(total), mixed.shape).T[:8, :]
        for at, k in enumerate(ks):
            mine = slice(at * rows, (at + 1) * rows)
            out = piece(osend.at[k, i], m)
            out[...] = mixed[mine].reshape(out.shape)
            lsend[k, i, m, :, :rows] = log[:, mine]

    o_in = {}

    def send_back(k, i, m, slot, dev):
        at = (slot, i, m)
        lanes = pl.ds(0, rows_of(m))
        o_in[at] = [
            go(remote(piece(osend.at[k, i], m), piece(orecv.at[slot, i], m), os_sem.at[at], or_sem.at[at], dev)),
            go(remote(lsend.at[k, i, m, :, lanes], lrecv.at[slot, i, m, :, lanes], ls_sem.at[at], lr_sem.at[at], dev)),
        ]

    def merged(i, m, parts):
        rows = rows_of(m)
        logs = [log[i, m, :, :rows] for _, log in parts]
        peak = functools.reduce(jnp.maximum, logs)
        shares = [jnp.exp2(log - peak) for log in logs]
        total = functools.reduce(jnp.add, shares)
        mixed = jnp.zeros((rows, DH), F32)
        for share, (out, _) in zip(shares, parts):
            column = jnp.concatenate([share / total] * (DH // 8), axis=0).T
            mixed += column * piece(out.at[i], m)[...].reshape(rows, DH).astype(F32)
        return mixed.astype(BF16), peak + jnp.log2(total)

    def cross(i, m):
        for copy in o_in[3, i, m]:
            copy.wait_recv()
        mixed, log = merged(i, m, [(osend.at[2], lsend.at[2]), (orecv.at[3], lrecv.at[3])])
        out = piece(osend.at[4, i], m)
        out[...] = mixed.reshape(out.shape)
        lsend[4, i, m, :, : rows_of(m)] = log
        send_back(4, i, m, 2, to_z(2))

    a_in = {}

    def merge(i, m):
        for k in (1, 2):
            for copy in o_in[k, i, m]:
                copy.wait_recv()
        mixed, _ = merged(
            i, m, [(osend.at[0], lsend.at[0])] + [(orecv.at[k], lrecv.at[k]) for k in (1, 2)]
        )
        for at, c in enumerate(parts_of(m)):
            for half in range(2):
                first = at * CHUNK + half * CHUNK // 2
                att[half, i, int(m == 2), c] = mixed[first : first + CHUNK // 2]
        a_in[i, m] = go(
            remote(piece(att.at[1, i], m), piece(attx.at[i], m), as_sem.at[i, m], ar_sem.at[i, m], twin)
        )

    def outgoing(i, m):
        for k in (3, 1):
            for n in (0, 1) if m == 3 else (m,):
                q_in[k, i, n].wait_recv()
        for ks in ((3,), (1,)):
            attend(ks, i, m)
            for k in ks:
                send_back(k, i, m, k, to_z(1))

    def staying(i, m):
        for ks in ((2, 0),) if m >= 2 else ((2,), (0,)):
            attend(ks, i, m)

    p_in = {}

    def project_out(m):
        for i in range(H):
            n = 3 if m < 2 and i < H - 1 else m
            if (n, m) != (3, 1):
                a_in[i, n].wait_recv()
        rows = rows_of(m) // 2
        both = jnp.concatenate(
            [
                jnp.concatenate([piece(ref.at[i], m)[...].reshape(rows, DH) for i in range(H)], axis=1)
                for ref in (att.at[0], attx)
            ],
            axis=0,
        )
        for side in range(2):

            def some(t, carry, side=side):
                cols = pl.ds(pl.multiple_of(side * WIDE + t * tile, tile), tile)
                got = jnp.dot(both, wo[:, cols], preferred_element_type=F32)
                got = (gate[0:1, cols] * got[:rows] + gatex[0:1, cols] * got[rows:]).astype(BF16)
                for at, c in enumerate(parts_of(m)):
                    mine = got[at * CHUNK // 2 : (at + 1) * CHUNK // 2].reshape(NY, PART, tile)
                    psend[side, :, m // 2, c, :, pl.ds(pl.multiple_of(t * tile, tile), tile)] = mine
                return carry

            lax.fori_loop(0, WIDE // tile, some, 0)
            for d in (2, 1, 3):
                at = (m, side, d)
                p_in[at] = go(
                    remote(
                        piece(psend.at[side, d], m), piece(precv.at[side, d], m), ps_sem.at[at], pr_sem.at[at], to_y(NY - d)
                    )
                )

    def summed(m, side):
        total = piece(psend.at[side, 0], m)[...].astype(F32)
        for d in (1, 3, 2):
            p_in[m, side, d].wait_recv()
            total += piece(precv.at[side, d], m)[...].astype(F32)
        return total

    def arrived(i):
        for m in range(3):
            for side in range(2):
                kv_in[2, i, m, side].wait_recv()

    def ready():
        load_o.wait()
        gate_copy.wait_recv()

    steps = [(0, 2), (1, 2), (2, 2), (0, 3), (1, 3), (2, 0), (2, 1)]
    during = {(2, 0): [lambda: project_out(2)]}
    after = {
        (0, 3): [lambda: merge(0, 2), lambda: merge(1, 2)],
        (1, 3): [ready, lambda: merge(2, 2)],
        (2, 0): [lambda: merge(0, 3)],
        (2, 1): [lambda: merge(1, 3)],
    }
    for at, (i, m) in enumerate(steps):
        if m == 2:
            arrived(i)
        outgoing(i, m)
        if at:
            cross(*steps[at - 1])
        for task in during.get((i, m), []):
            task()
        staying(i, m)
        for task in after.get((i, m), []):
            task()
    merge(2, 0)
    cross(*steps[-1])
    project_out(0)

    z_in, f_in = [], {}
    for side in range(2):
        zsend[side] = summed(2, side).astype(BF16)
        z_in.append(go(remote(zsend.at[side], zrecv.at[side], zs_sem.at[side], zr_sem.at[side], far)))
    merge(2, 1)
    project_out(1)
    for m in range(2):
        for side in range(2):
            whole = summed(m, side)
            if m == 0:
                z_in[side].wait_recv()
            whole += zrecv[side, m].astype(F32)
            fin[m, side] = whole
            f_in[m, side] = go(
                remote(fin.at[m, side], finx.at[m, side], fs_sem.at[m, side], fr_sem.at[m, side], twin)
            )
            rows = pl.ds(pl.multiple_of(b * ROWS + m * PART, PART), PART)
            out_ref[rows, side * WIDE : (side + 1) * WIDE] = whole
    for m in range(2):
        for side in range(2):
            f_in[m, side].wait_recv()
            rows = pl.ds(pl.multiple_of((1 - b) * ROWS + m * PART, PART), PART)
            out_ref[rows, side * WIDE : (side + 1) * WIDE] = finx[m, side]

    for copy in sends:
        copy.wait_send()

    @pl.when(inner)
    def _():
        for copy in relays:
            copy.wait_send()
        for m in range(3):
            for i in range(H):
                q_in[3, i, m].wait_send()


def guided(latent, modulation, wq, wo):
    dma = pltpu.SemaphoreType.DMA
    vmem = pltpu.VMEM
    scratch = [
        vmem((H, D, 3 * DH), BF16),
        vmem((H * DH, D), BF16),
        vmem((2, 2, 2, NY, PART, D), BF16),
        vmem((2, 2 * CHUNK, D), BF16),
        vmem((NZ, H, 2, 2, CHUNK, DH), BF16),
        vmem((NX, H, 2, 2, 2, DH, CHUNK), BF16),
        vmem((NZ + 1, H, 2, 2, CHUNK, DH), BF16),
        vmem((NZ, H, 2, 2, CHUNK, DH), BF16),
        vmem((NZ + 1, H, 4, 8, 2 * CHUNK), F32),
        vmem((NZ, H, 4, 8, 2 * CHUNK), F32),
        vmem((2, H, 2, 2, CHUNK // 2, DH), BF16),
        vmem((H, 2, 2, CHUNK // 2, DH), BF16),
        vmem((8, D), F32),
        vmem((8, D), F32),
        vmem((2, NY, 2, 2, PART, WIDE), BF16),
        vmem((2, NY, 2, 2, PART, WIDE), BF16),
        vmem((2, 2, PART, WIDE), BF16),
        vmem((2, 2, PART, WIDE), BF16),
        vmem((2, 2, PART, WIDE), F32),
        vmem((2, 2, PART, WIDE), F32),
        dma((2,)),
        dma((2, 2, 2, NY)), dma((2, 2, 2, NY)), dma((2, 2, 2, 2)),
        dma((2,)),
        dma((NZ, H, 3)), dma((NZ, H, 3)), dma((H, 3)),
        dma((NX, H, 3)), dma((NX, H, 3)), dma((2, H, 3, 2)),
        dma((NZ, H, 4)), dma((NZ, H, 4)),
        dma((NZ, H, 4)), dma((NZ, H, 4)),
        dma((H, 4)), dma((H, 4)),
        dma((3, 2, NY)), dma((3, 2, NY)),
        dma((2,)), dma((2,)),
        dma((2, 2)), dma((2, 2)),
    ]
    held = pl.BlockSpec(memory_space=pltpu.VMEM)
    left = pl.BlockSpec(memory_space=pl.ANY)
    return pl.pallas_call(
        kernel,
        out_shape=jax.ShapeDtypeStruct(latent.shape, F32),
        in_specs=[held, held, left, left],
        out_specs=held,
        scratch_shapes=scratch,
        compiler_params=pltpu.CompilerParams(
            collective_id=0, has_side_effects=True, vmem_limit_bytes=60 * 1024 * 1024
        ),
    )(latent, modulation, wq, wo)


def shards(latent, modulation, w_qkv, w_out, timestep):
    wq = jnp.transpose(w_qkv, (1, 0, 2))
    wo = w_out.reshape(H * DH, D)
    change = guided(latent, jnp.transpose(modulation, (1, 0, 2)), wq, wo)
    moment = timestep[0].astype(F32)
    sigma_now = sigma_at(moment)
    step_size = sigma_at(moment + 1.0) - sigma_now
    velocity = latent + change
    return (latent + step_size * velocity, latent - sigma_now * velocity)


def solution(mesh):
    placed = (
        P(("seq", "head"), None),
        P("branch", None, None),
        P(None, "head", None),
        P("head", None, None),
        P(),
    )
    return jax.shard_map(
        shards,
        mesh=mesh,
        in_specs=placed,
        out_specs=(P(("seq", "head"), None), P(("seq", "head"), None)),
        check_vma=False,
    )
```

profile of v0, /device:TPU:7, one launch (start us, length us, event | category | flops | bytes accessed | tf_op | source)
XLA Modules:
  0.0 113.5 jit_solution(16102361112531744252)
XLA Ops:
  0.6 0.0 copy-start
  1.5 109.6 %shard_map.68 = f32[64,3072]{1,0:T(8,128)} custom-call(f32[64,3072]{1,0:T(8,128)} %lat_ref.1, f32[3,1,3072]{2,1,0:T(1,128)} %bitcast.7, bf16[3,3072,384]{2,1,0:T(8,128)(2,1)} %bitcast.5, bf16[384,3072]{1,0:T(8,128)(2,1)} %bitcast.6), custom_call_target="tpu_custom_call" | custom-call | tf_op jit(solution)/shard_map/pallas_call | solution.py:512
  111.0 0.0 copy-done
  111.0 2.5 %multiply_subtract_fusion = (f32[64,3072]{1,0:T(8,128)}, f32[64,3072]{1,0:T(8,128)}) fusion(f32[64,3072]{1,0:T(8,128)S(1)} %copy-done, f32[]{:T(128)} %bitcast.1, f32[64,3072]{1,0:T(8,128)} %shard_map.68, f32[]{:T(128)S(6)} %sub.19), kind=kLoop, calls=%fused_computation | loop fusion | flops 983040 | bytes 3145736 | tf_op jit(solution)/shard_map/sub | solution.py:532
Async XLA Ops:
  0.6 110.4 %copy-start = (f32[64,3072]{1,0:T(8,128)S(1)}, f32[64,3072]{1,0:T(8,128)}, u32[]{:S(2)}) copy-start(f32[64,3072]{1,0:T(8,128)} %lat_ref.1) | copy-start | bytes 2359300
where the time goes:
time: 114 us
  Pallas kernels  110 us (96%)
  other arithmetic  2.47 us (2%)
  between operations  1.47 us (1%)
    pallas_call x1, Pallas kernels, guided(): pl.pallas_call(kernel, out_shape=jax.ShapeDtypeStruct(latent.shape, F32),...  110 us
    sub x1, other arithmetic, shards(): return (latent + step_size * velocity, latent - sigma_now * velocity)  2.47 us

commit v1 on v0

--- a/solution.py
+++ b/solution.py
@@ -103,14 +103,7 @@
     def modulate(dz, c, half, dy):
         rows = pl.ds(((c * 2 + half) * NY + dy) * PART, PART)
 
-        def some(t, carry):
-            cols = pl.ds(pl.multiple_of(t * tile, tile), tile)
-            nm[dz, rows, cols] = (
-                xh[dz, c, half, dy, :, cols].astype(F32) * (1.0 + mod_ref[1, :, cols]) + mod_ref[0, :, cols]
-            ).astype(BF16)
-            return carry
-
-        lax.fori_loop(0, D // tile, some, 0)
+        nm[dz, rows, :] = (xh[dz, c, half, dy].astype(F32) * (1.0 + mod_ref[1]) + mod_ref[0]).astype(BF16)
 
     tile = 512
     x_in = {}
@@ -387,7 +380,7 @@
                     psend[side, :, m // 2, c, :, pl.ds(pl.multiple_of(t * tile, tile), tile)] = mine
                 return carry
 
-            lax.fori_loop(0, WIDE // tile, some, 0)
+            lax.fori_loop(0, WIDE // tile, some, 0, unroll=True)
             for d in (2, 1, 3):
                 at = (m, side, d)
                 p_in[at] = go(

time: 114 us -> 111 us (0.974)
  Pallas kernels: 110 us -> 106 us
    pallas_call x1, Pallas kernels: 110 us -> 106 us  [guided(): pl.pallas_call(kernel, out_shape=jax.ShapeDtypeStruct(latent.shape, F32),...]
where the time goes in v1:
time: 111 us; the launch traced here: 110 us
  Pallas kernels  106 us (95%)
  other arithmetic  2.47 us (2%)
  between operations  1.47 us (1%)
    pallas_call x1, Pallas kernels, guided(): pl.pallas_call(kernel, out_shape=jax.ShapeDtypeStruct(latent.shape, F32),...  106 us
    sub x1, other arithmetic, shards(): return (latent + step_size * velocity, latent - sigma_now * velocity)  2.47 us

profile of v1, /device:TPU:7, one launch (start us, length us, event | category | flops | bytes accessed | tf_op | source)
XLA Modules:
  0.0 109.9 jit_solution(13449571267457747846)
XLA Ops:
  0.6 0.0 copy-start
  1.5 105.9 %shard_map.68 = f32[64,3072]{1,0:T(8,128)} custom-call(f32[64,3072]{1,0:T(8,128)} %lat_ref.1, f32[3,1,3072]{2,1,0:T(1,128)} %bitcast.7, bf16[3,3072,384]{2,1,0:T(8,128)(2,1)} %bitcast.5, bf16[384,3072]{1,0:T(8,128)(2,1)} %bitcast.6), custom_call_target="tpu_custom_call" | custom-call | tf_op jit(solution)/shard_map/pallas_call | solution.py:505
  107.4 0.0 copy-done
  107.4 2.5 %multiply_subtract_fusion = (f32[64,3072]{1,0:T(8,128)}, f32[64,3072]{1,0:T(8,128)}) fusion(f32[64,3072]{1,0:T(8,128)S(1)} %copy-done, f32[]{:T(128)} %bitcast.1, f32[64,3072]{1,0:T(8,128)} %shard_map.68, f32[]{:T(128)S(6)} %sub.19), kind=kLoop, calls=%fused_computation | loop fusion | flops 983040 | bytes 3145736 | tf_op jit(solution)/shard_map/sub | solution.py:525
Async XLA Ops:
  0.6 106.8 %copy-start = (f32[64,3072]{1,0:T(8,128)S(1)}, f32[64,3072]{1,0:T(8,128)}, u32[]{:S(2)}) copy-start(f32[64,3072]{1,0:T(8,128)} %lat_ref.1) | copy-start | bytes 2359300
